TPU v7x, 256 devices: a whole 4x4x8 slice. The times are simulated.
256 devices in a mesh: grp: 8 (over y, z_hi), ep: 32 (over x, z_lo, core).
Axes of the slice: x: 4, y: 4, z: 8 (z_hi: 2, z_lo: 4; z = z_hi * 4 + z_lo), core: 2. Of those that a mesh axis runs over, the one named last changes fastest.
Arguments:
- tokens: bfloat16 [4096, 5120], P('ep', 'grp'), may hold values from -6 to 6
- out_grad: bfloat16 [4096, 5120], P('ep', 'grp'), may hold values from -1.5 to 1.5
- expert_ids: int32 [4096, 6], P('ep'), may hold values from 0 to 23, all different within a row; in each aligned block of 128 rows (0 to 127, 128 to 255, ...) at most 40 rows name the same one
- route_probs: bfloat16 [4096, 6], P('ep'), may hold values from 0.049804688 to 0.59765625
- slot_expert: int32 [32], replicated, may hold values from 0 to 23, as said below
- w_gate: bfloat16 [32, 5120, 1024], P('ep', 'grp'), as said below
- w_up: bfloat16 [32, 5120, 1024], P('ep', 'grp'), as said below
- w_down: bfloat16 [32, 5120, 1024], P('ep', 'grp'), as said below
Outputs:
- in_grad: bfloat16 [4096, 5120], P('ep', 'grp')
- grad_gate: bfloat16 [32, 5120, 1024], P('ep', 'grp')
- grad_up: bfloat16 [32, 5120, 1024], P('ep', 'grp')
- grad_down: bfloat16 [32, 5120, 1024], P('ep', 'grp')
Inputs may be any that keep to these rules, and one draw needn't show every extreme that they name: `expert_ids`: in the rows of one index of ep, no expert is named by more than 40 tokens; some expert is named by exactly 40 in some block. `slot_expert`: every expert 0 to 23 is held by at least one of the 32 slots. `w_gate`: slots that hold the same expert hold equal weights. `w_up`: slots that hold the same expert hold equal weights. `w_down`: slots that hold the same expert hold equal weights.
All inputs are finite; a program needn't handle non-finite values.
Results may differ from a plain program's by a relative error of at most 0.03.
Values may be sent and summed in bfloat16 or wider, within the bound.
No kernel may reach another device: no remote copies, remote signals or barrier semaphores. Data moves between devices by JAX's collectives and lax.ppermute only.
A program may use at most 128 MiB of HBM per device.

v0:
```python
import jax
import jax.numpy as jnp
from jax import lax
from jax.sharding import PartitionSpec as P


def activate(gate, up_sum, grad_hidden):
    sigma = jax.nn.sigmoid(gate)
    swish = gate * sigma
    hidden = (swish * up_sum).astype(jnp.bfloat16)
    grad_up = (grad_hidden * swish).astype(jnp.bfloat16)
    grad_gate = (grad_hidden * up_sum * sigma * (1.0 + gate * (1.0 - sigma))).astype(jnp.bfloat16)
    return (hidden, grad_gate, grad_up)


def per_device(tokens, out_grad, expert_ids, route_probs, slot_expert, w_gate, w_up, w_down):
    tok_count, width_part = tokens.shape
    top_count = expert_ids.shape[1]
    num_slots = lax.axis_size("ep")
    in_flight = 3 * num_slots // 4
    capacity = (30 * tok_count + 4 * in_flight - 1) // (4 * in_flight)
    slot_rows = num_slots * capacity
    slot_ids = jnp.arange(num_slots, dtype=jnp.int32)
    same_expert = (slot_expert[:, None] == slot_expert[None, :]).astype(jnp.int32)
    earlier = (slot_ids[:, None] > slot_ids[None, :]).astype(jnp.int32)
    replica_rank = jnp.sum(same_expert * earlier, axis=1)
    flat_ids = expert_ids.reshape(-1)
    hosting = flat_ids[:, None] == slot_expert[None, :]
    replicas = jnp.sum(hosting.astype(jnp.int32), axis=1)
    replica = lax.axis_index("ep") % replicas
    chosen = (hosting & (replica_rank[None, :] == replica[:, None])).astype(jnp.int32)
    target = jnp.sum(chosen * slot_ids[None, :], axis=1)
    position = jnp.sum((jnp.cumsum(chosen, axis=0) - 1) * chosen, axis=1)
    buffer_index = target * capacity + position
    send_tokens = (
        jnp.zeros((slot_rows, width_part), jnp.bfloat16)
        .at[buffer_index]
        .set(jnp.repeat(tokens, top_count, axis=0))
    )
    send_grads = (
        jnp.zeros((slot_rows, width_part), jnp.bfloat16)
        .at[buffer_index]
        .set(jnp.repeat(out_grad, top_count, axis=0))
    )
    send_probs = jnp.zeros((slot_rows,), jnp.bfloat16).at[buffer_index].set(route_probs.reshape(-1))
    recv_tokens, recv_grads, recv_probs = (
        lax.all_to_all(
            send_tokens.reshape(num_slots, capacity, width_part),
            "ep",
            split_axis=0,
            concat_axis=0,
            tiled=True,
        ),
        lax.all_to_all(
            send_grads.reshape(num_slots, capacity, width_part),
            "ep",
            split_axis=0,
            concat_axis=0,
            tiled=True,
        ),
        lax.all_to_all(
            send_probs.reshape(num_slots, capacity), "ep", split_axis=0, concat_axis=0, tiled=True
        ),
    )
    inputs = recv_tokens.reshape(slot_rows, width_part)
    scaled = (
        recv_probs.reshape(slot_rows, 1).astype(jnp.float32)
        * recv_grads.reshape(slot_rows, width_part)
    ).astype(jnp.bfloat16)
    gate_rows = w_gate[0]
    up_rows = w_up[0]
    down_rows = w_down[0]
    gate_part = jnp.dot(inputs, gate_rows, preferred_element_type=jnp.float32)
    up_part = jnp.dot(inputs, up_rows, preferred_element_type=jnp.float32)
    hidden_part = jnp.dot(scaled, down_rows, preferred_element_type=jnp.float32)
    gate, up_sum, grad_hidden = (
        lax.psum(gate_part.astype(jnp.bfloat16), "grp").astype(jnp.float32),
        lax.psum(up_part.astype(jnp.bfloat16), "grp").astype(jnp.float32),
        lax.psum(hidden_part.astype(jnp.bfloat16), "grp").astype(jnp.float32),
    )
    hidden, grad_gate, grad_up = activate(gate, up_sum, grad_hidden)
    part_gate = jnp.dot(inputs.T, grad_gate, preferred_element_type=jnp.float32).astype(
        jnp.bfloat16
    )
    part_up = jnp.dot(inputs.T, grad_up, preferred_element_type=jnp.float32).astype(jnp.bfloat16)
    part_down = jnp.dot(scaled.T, hidden, preferred_element_type=jnp.float32).astype(jnp.bfloat16)
    row_grad = (
        jnp.dot(grad_gate, gate_rows.T, preferred_element_type=jnp.float32)
        + jnp.dot(grad_up, up_rows.T, preferred_element_type=jnp.float32)
    ).astype(jnp.bfloat16)
    returned = lax.all_to_all(
        row_grad.reshape(num_slots, capacity, width_part),
        "ep",
        split_axis=0,
        concat_axis=0,
        tiled=True,
    )
    gathered = returned.reshape(slot_rows, width_part)[buffer_index]
    in_grad = jnp.sum(
        gathered.astype(jnp.float32).reshape(tok_count, top_count, width_part), axis=1
    ).astype(jnp.bfloat16)
    stacked = jnp.stack([part_gate, part_up, part_down])[None]
    mixing = same_expert.astype(jnp.bfloat16)
    mixed = jnp.einsum(
        "st,tkrh->skrh",
        mixing,
        lax.all_to_all(stacked, "ep", split_axis=2, concat_axis=0, tiled=True),
        preferred_element_type=jnp.float32,
    ).astype(jnp.bfloat16)
    summed = lax.all_to_all(mixed, "ep", split_axis=0, concat_axis=2, tiled=True)
    return (in_grad, summed[:, 0], summed[:, 1], summed[:, 2])


def solution(mesh):
    return jax.shard_map(
        per_device,
        mesh=mesh,
        in_specs=(
            P("ep", "grp"),
            P("ep", "grp"),
            P("ep", None),
            P("ep", None),
            P(),
            P("ep", "grp", None),
            P("ep", "grp", None),
            P("ep", "grp", None),
        ),
        out_specs=(
            P("ep", "grp"),
            P("ep", "grp", None),
            P("ep", "grp", None),
            P("ep", "grp", None),
        ),
        check_vma=False,
    )
```

profile of v0, /device:TPU:1, one launch (start us, length us, event | category | flops | bytes accessed | tf_op | source)
XLA Modules:
  0.0 1098.0 jit_solution(3408724642398284460)
XLA Ops:
  14.8 8.6 scatter_custom_fusion
  24.2 10.0 all-to-all-start
  36.4 7.5 scatter_custom_fusion.2
  43.9 8.1 all-to-all-start.2
  53.3 7.4 scatter_custom_fusion.1
  60.7 31.3 %all-to-all-done.2 = bf16[32,40,640]{2,1,0:T(8,128)(2,1)} async-done(((bf16[32,40,640]{2,1,0:T(8,128)(2,1)}), bf16[32,40,640]{2,1,0:T(8,128)(2,1)}, u32[]{:S(2)}, u32[]{:S(2)}) %all-to-all-start.2) | async-done | bytes 1638432 | tf_op jit(solution)/shard_map/all_to_all | solution.py:47
  92.1 4.2 all-to-all-start.1
  96.4 5.3 convolution_convert_fusion
  101.7 5.2 convolution_convert_fusion.1
  106.9 29.8 %all-to-all-done.1 = bf16[32,40,640]{2,1,0:T(8,128)(2,1)S(1)} async-done(((bf16[32,40,640]{2,1,0:T(8,128)(2,1)}), bf16[32,40,640]{2,1,0:T(8,128)(2,1)S(1)}, u32[]{:S(2)}, u32[]{:S(2)}) %all-to-all-start.1) | async-done | bytes 1638432 | tf_op jit(solution)/shard_map/all_to_all | solution.py:54
  138.0 3.7 convolution_convert_fusion.2
  143.4 629.0 %all-reduce.3.cloned.1.call-done = (bf16[1280,1024]{1,0:T(8,128)(2,1)}, bf16[1280,1024]{1,0:T(8,128)(2,1)}, bf16[1280,1024]{1,0:T(8,128)(2,1)}) async-done(((bf16[1280,1024]{1,0:T(8,128)(2,1)}, bf16[1280,1024]{1,0:T(8,128)(2,1)}, bf16[1280,1024]{1,0:T(8,128)(2,1)}), (bf16[1280,1024]{1,0:T(8,128)(2,1)}, bf16[1280,1024]{1,0:T(8,128)(2,1)}, bf16[1280,1024]{1,0:T(8,128)(2,1)})) %all-reduce.3.cloned.1.call-update) | async-done | bytes 7864336 | tf_op jit(solution)/shard_map/psum | solution.py:78
  772.4 5.3 fusion.24
  777.7 3.2 fusion
  781.0 4.6 fusion.23
  785.6 3.3 fusion.22
  789.4 5.7 copy.24
  795.1 6.4 all-to-all-start.4
  801.6 4.1 fusion.27
  805.7 3.5 fusion.13
  809.2 109.1 %all-to-all-done.4 = bf16[1,3,640,1024]{3,1,0,2:T(4,128)(2,1)} async-done(((bf16[1,3,640,1024]{3,1,0,2:T(4,128)(2,1)}), bf16[1,3,640,1024]{3,1,0,2:T(4,128)(2,1)}, u32[]{:S(2)}, u32[]{:S(2)}) %all-to-all-start.4) | async-done | bytes 3932192 | tf_op jit(solution)/shard_map/all_to_all | solution.py:107
  918.3 4.8 all-to-all-start.3
  923.2 7.9 fusion.16
  931.1 4.4 copy.27
  935.5 28.0 %all-to-all-done.3 = bf16[32,40,640]{2,1,0:T(8,128)(2,1)S(1)} async-done(((bf16[32,40,640]{2,1,0:T(8,128)(2,1)}), bf16[32,40,640]{2,1,0:T(8,128)(2,1)S(1)}, u32[]{:S(2)}, u32[]{:S(2)}) %all-to-all-start.3) | async-done | bytes 1638432 | tf_op jit(solution)/shard_map/all_to_all | solution.py:91
  963.5 5.7 all-to-all-start.5
  969.2 3.4 gather_fusion
  972.6 2.1 gather.6
  976.2 98.6 %all-to-all-done.5 = bf16[32,3,20,1024]{3,2,1,0:T(8,128)(2,1)} async-done(((bf16[32,3,20,1024]{3,2,1,0:T(8,128)(2,1)}), bf16[32,3,20,1024]{3,2,1,0:T(8,128)(2,1)}, u32[]{:S(2)}, u32[]{:S(2)}) %all-to-all-start.5) | async-done | bytes 3932192 | tf_op jit(solution)/shard_map/all_to_all | solution.py:110
  1074.8 5.2 copy.28
  1080.0 6.9 all_to_all.53
  1086.9 4.1 slice_bitcast_fusion
  (56 shorter events, 17.0 us)
Async XLA Ops:
  7.2 89.2 %copy-start = (bf16[1,640,1024]{2,1,0:T(8,128)(2,1)S(1)}, bf16[1,640,1024]{2,1,0:T(8,128)(2,1)}, u32[]{:S(2)}) copy-start(bf16[1,640,1024]{2,1,0:T(8,128)(2,1)} %param.13) | copy-start | bytes 3932164
  24.2 19.7 %all-to-all-start = ((bf16[32,1,40]{2,1,0:T(2,128)(2,1)}), bf16[32,1,40]{2,1,0:T(2,128)(2,1)S(1)}, u32[]{:S(2)}, u32[]{:S(2)}) async-start(bf16[32,1,40]{2,1,0:T(2,128)(2,1)} %all_to_all.54), calls=%async_computation | async-start | bytes 32768 | tf_op jit(solution)/shard_map/all_to_all | solution.py:61
  36.4 15.6 %copy-start.7 = (bf16[128,640]{1,0:T(8,128)(2,1)S(1)}, bf16[128,640]{1,0:T(8,128)(2,1)}, u32[]{:S(2)}) copy-start(bf16[128,640]{1,0:T(8,128)(2,1)} %param.9) | copy-start | bytes 491524
  43.9 48.2 %all-to-all-start.2 = ((bf16[32,40,640]{2,1,0:T(8,128)(2,1)}), bf16[32,40,640]{2,1,0:T(8,128)(2,1)}, u32[]{:S(2)}, u32[]{:S(2)}) async-start(bf16[32,40,640]{2,1,0:T(8,128)(2,1)} %bitcast.6), calls=%async_computation.2 | async-start | bytes 3276800 | tf_op jit(solution)/shard_map/all_to_all | solution.py:47
  92.1 44.6 %all-to-all-start.1 = ((bf16[32,40,640]{2,1,0:T(8,128)(2,1)}), bf16[32,40,640]{2,1,0:T(8,128)(2,1)S(1)}, u32[]{:S(2)}, u32[]{:S(2)}) async-start(bf16[32,40,640]{2,1,0:T(8,128)(2,1)} %bitcast.88), calls=%async_computation.1 | async-start | bytes 3276800 | tf_op jit(solution)/shard_map/all_to_all | solution.py:54
  96.3 676.1 %all-reduce.3.cloned.1.call-start = ((), (), s32[]{:S(2)}) async-start(), calls=%async_computation.6 | async-start | bytes 15728640 | tf_op jit(solution)/shard_map/psum | solution.py:78
  96.4 5.3 copy-start.10
  136.7 1.3 copy-start.9
  772.4 5.3 copy-start.1
  772.4 5.3 copy-start.2
  772.4 5.3 copy-start.3
  781.0 4.6 copy-start.4
  781.0 4.6 copy-start.6
  795.1 123.2 %all-to-all-start.4 = ((bf16[1,3,640,1024]{3,1,0,2:T(4,128)(2,1)}), bf16[1,3,640,1024]{3,1,0,2:T(4,128)(2,1)}, u32[]{:S(2)}, u32[]{:S(2)}) async-start(bf16[1,3,640,1024]{3,1,0,2:T(4,128)(2,1)} %copy.24), calls=%async_computation.4 | async-start | bytes 10485760 | tf_op jit(solution)/shard_map/all_to_all | solution.py:107
  801.5 4.2 copy-start.5
  801.6 4.2 copy-start.11
  809.2 113.9 %copy-start.8 = (s32[32]{0:T(128)S(1)}, s32[32]{0:T(128)}, u32[]{:S(2)}) copy-start(s32[32]{0:T(128)} %param.12) | copy-start | bytes 388
  918.3 45.2 %all-to-all-start.3 = ((bf16[32,40,640]{2,1,0:T(8,128)(2,1)}), bf16[32,40,640]{2,1,0:T(8,128)(2,1)S(1)}, u32[]{:S(2)}, u32[]{:S(2)}) async-start(bf16[32,40,640]{2,1,0:T(8,128)(2,1)} %bitcast.89), calls=%async_computation.3 | async-start | bytes 3276800 | tf_op jit(solution)/shard_map/all_to_all | solution.py:91
  963.5 111.3 %all-to-all-start.5 = ((bf16[32,3,20,1024]{3,2,1,0:T(8,128)(2,1)}), bf16[32,3,20,1024]{3,2,1,0:T(8,128)(2,1)}, u32[]{:S(2)}, u32[]{:S(2)}) async-start(bf16[32,3,20,1024]{3,2,1,0:T(8,128)(2,1)} %copy.27), calls=%async_computation.5 | async-start | bytes 9437184 | tf_op jit(solution)/shard_map/all_to_all | solution.py:110
Sparse Core Ops, SparseCore 0:
  141.8 630.5 all-reduce.2
where the time goes:
time: 1110 us; the launch traced here: 1100 us
  waiting for transfers between devices  926 us (83%)
  local copies, waits for them, and re-layouts  63 us (6%)
  matrix products  42.9 us (4%)
  starting transfers between devices  39.3 us (4%)
  between operations  14.5 us (1%)
  other arithmetic  12.4 us (1%)
    psum x1, waiting for transfers between devices, per_device(): lax.psum(up_part.astype(jnp.bfloat16), 'grp').astype(jnp.float32)  629 us
    all_to_all x1, waiting for transfers between devices, per_device(): lax.all_to_all(stacked, 'ep', split_axis=2, concat_axis=0, tiled=True)  109 us
    all_to_all x1, waiting for transfers between devices, per_device(): lax.all_to_all(mixed, 'ep', split_axis=0, concat_axis=2, tiled=True)  98.6 us
    all_to_all x1, waiting for transfers between devices, per_device(): lax.all_to_all(send_tokens.reshape(num_slots, capacity, width_part), 'ep'...  31.3 us
    all_to_all x1, waiting for transfers between devices, per_device(): lax.all_to_all(send_grads.reshape(num_slots, capacity, width_part), 'ep',...  29.8 us
    all_to_all x1, waiting for transfers between devices, per_device(): lax.all_to_all(row_grad.reshape(num_slots, capacity, width_part), 'ep', s...  28 us
  transfers between devices with their start and end apart: 7, of which 6 were waited for; matrix products, arithmetic and copies ran while one was open for 5% of the time, Pallas kernels for 0%

commit v1 on v0

--- a/solution.py
+++ b/solution.py
@@ -75,7 +75,7 @@
     hidden_part = jnp.dot(scaled, down_rows, preferred_element_type=jnp.float32)
     gate, up_sum, grad_hidden = (
         lax.psum(gate_part.astype(jnp.bfloat16), "grp").astype(jnp.float32),
-        lax.psum(up_part.astype(jnp.bfloat16), "grp").astype(jnp.float32),
+        jnp.sum(lax.all_gather(up_part.astype(jnp.bfloat16), "grp"), axis=0).astype(jnp.float32),
         lax.psum(hidden_part.astype(jnp.bfloat16), "grp").astype(jnp.float32),
     )
     hidden, grad_gate, grad_up = activate(gate, up_sum, grad_hidden)

time: 1110 us -> 1220 us (1.099)
  blocking collectives: 0 us -> 50.6 us
  waiting for transfers between devices: 926 us -> 955 us
  starting transfers between devices: 39.3 us -> 62.3 us
  other arithmetic: 12.4 us -> 25.5 us
    all_gather x0 -> x1, waiting for transfers between devices: none -> 166 us  [per_device(): lax.all_gather(up_part.astype(jnp.bfloat16), 'grp')]
    psum x1, waiting for transfers between devices: 629 us -> 508 us  [per_device(): lax.psum(hidden_part.astype(jnp.bfloat16), 'grp').astype(jnp.float32)]
    all_to_all x0 -> x1, blocking collectives: none -> 50.6 us  [per_device(): lax.all_to_all(send_tokens.reshape(num_slots, capacity, width_part), 'ep'...]
    all_to_all x1, starting transfers between devices: 4.23 us -> 41.9 us  [per_device(): lax.all_to_all(send_grads.reshape(num_slots, capacity, width_part), 'ep',...]
    all_to_all x1 -> x0, waiting for transfers between devices: 31.3 us -> none  [per_device(): lax.all_to_all(send_tokens.reshape(num_slots, capacity, width_part), 'ep'...]
    all_to_all x1, waiting for transfers between devices: 29.8 us -> 45.9 us  [per_device(): lax.all_to_all(send_grads.reshape(num_slots, capacity, width_part), 'ep',...]
    reduce_sum x0 -> x1, other arithmetic: none -> 13.4 us  [per_device(): jnp.sum(lax.all_gather(up_part.astype(jnp.bfloat16), 'grp'), axis=0)]
  transfers between devices with their start and end apart: 7 -> 7, of which waited for: 6 -> 6; matrix products, arithmetic and copies ran while one was open for 5% -> 6% of each run, Pallas kernels for 0% -> 0%
where the time goes in v1:
time: 1220 us; the launch traced here: 1210 us
  waiting for transfers between devices  955 us (78%)
  local copies, waits for them, and re-layouts  64.2 us (5%)
  starting transfers between devices  62.3 us (5%)
  blocking collectives  50.6 us (4%)
  matrix products  35.3 us (3%)
  other arithmetic  25.5 us (2%)
  between operations  14.8 us (1%)
    psum x1, waiting for transfers between devices, per_device(): lax.psum(hidden_part.astype(jnp.bfloat16), 'grp').astype(jnp.float32)  508 us
    all_gather x1, waiting for transfers between devices, per_device(): lax.all_gather(up_part.astype(jnp.bfloat16), 'grp')  166 us
    all_to_all x1, waiting for transfers between devices, per_device(): lax.all_to_all(stacked, 'ep', split_axis=2, concat_axis=0, tiled=True)  109 us
    all_to_all x1, waiting for transfers between devices, per_device(): lax.all_to_all(mixed, 'ep', split_axis=0, concat_axis=2, tiled=True)  98.6 us
    all_to_all x1, blocking collectives, per_device(): lax.all_to_all(send_tokens.reshape(num_slots, capacity, width_part), 'ep'...  50.6 us
    all_to_all x1, waiting for transfers between devices, per_device(): lax.all_to_all(send_grads.reshape(num_slots, capacity, width_part), 'ep',...  45.9 us
    all_to_all x1, starting transfers between devices, per_device(): lax.all_to_all(send_grads.reshape(num_slots, capacity, width_part), 'ep',...  41.9 us
    all_to_all x1, waiting for transfers between devices, per_device(): lax.all_to_all(row_grad.reshape(num_slots, capacity, width_part), 'ep', s...  28 us
  transfers between devices with their start and end apart: 7, of which 6 were waited for; matrix products, arithmetic and copies ran while one was open for 6% of the time, Pallas kernels for 0%

profile of v1, /device:TPU:1, one launch (start us, length us, event | category | flops | bytes accessed | tf_op | source)
XLA Modules:
  0.0 1207.5 jit_solution(3428191825310815043)
XLA Ops:
  16.1 6.6 scatter_custom_fusion.2
  22.8 50.6 %all_to_all.61 = bf16[32,40,640]{2,1,0:T(8,128)(2,1)S(1)} all-to-all(bf16[32,40,640]{2,1,0:T(8,128)(2,1)S(1)} %bitcast.91), channel_id=1, replica_groups=mesh['grp'=8,'ep'=32] {'ep'}, dimensions={0} | all-to-all | bytes 3276800 | tf_op jit(solution)/shard_map/all_to_all | solution.py:47
  74.6 3.7 convolution_convert_fusion.1
  79.2 8.6 scatter_custom_fusion
  88.6 4.2 all-to-all-start
  94.1 7.6 scatter_custom_fusion.1
  101.7 41.9 %all-to-all-start.1 = ((bf16[32,40,640]{2,1,0:T(8,128)(2,1)}), bf16[32,40,640]{2,1,0:T(8,128)(2,1)S(1)}, u32[]{:S(2)}, u32[]{:S(2)}) async-start(bf16[32,40,640]{2,1,0:T(8,128)(2,1)} %bitcast.90), calls=%async_computation.1 | async-start | bytes 3276800 | tf_op jit(solution)/shard_map/all_to_all | solution.py:54
  143.7 45.9 %all-to-all-done.1 = bf16[32,40,640]{2,1,0:T(8,128)(2,1)S(1)} async-done(((bf16[32,40,640]{2,1,0:T(8,128)(2,1)}), bf16[32,40,640]{2,1,0:T(8,128)(2,1)S(1)}, u32[]{:S(2)}, u32[]{:S(2)}) %all-to-all-start.1) | async-done | bytes 1638432 | tf_op jit(solution)/shard_map/all_to_all | solution.py:54
  191.1 3.7 convolution_convert_fusion
  194.8 3.8 convolution_convert_fusion.2
  200.3 165.5 %all-gather.3.cloned.1.call-done = bf16[10240,1024]{1,0:T(8,128)(2,1)} async-done(((bf16[1280,1024]{1,0:T(8,128)(2,1)}), bf16[10240,1024]{1,0:T(8,128)(2,1)}) %all-gather.3.cloned.1.call-update) | async-done | bytes 20971536 | tf_op jit(solution)/shard_map/all_gather | solution.py:78
  365.8 13.4 %reduce_sum.67 = bf16[1280,1024]{1,0:T(8,128)(2,1)} reduce(bf16[8,1280,1024]{2,1,0:T(8,128)(2,1)} %bitcast.89, bf16[]{:T(256)} %constant.11.clone.1), dimensions={0}, to_apply=%region_10.11 | reduce | flops 9175040 | bytes 23592962 | tf_op jit(solution)/shard_map/reduce_sum | solution.py:78
  379.2 507.5 %all-reduce.3.cloned.1.call-done = (bf16[1280,1024]{1,0:T(8,128)(2,1)}, bf16[1280,1024]{1,0:T(8,128)(2,1)}) async-done(((bf16[1280,1024]{1,0:T(8,128)(2,1)}, bf16[1280,1024]{1,0:T(8,128)(2,1)}), (bf16[1280,1024]{1,0:T(8,128)(2,1)}, bf16[1280,1024]{1,0:T(8,128)(2,1)})) %all-reduce.3.cloned.1.call-update) | async-done | bytes 5242896 | tf_op jit(solution)/shard_map/psum | solution.py:79
  886.7 4.8 fusion.24
  891.6 3.0 fusion
  894.6 1.9 fusion.23
  899.4 5.7 copy.24
  905.1 5.7 all-to-all-start.4
  910.9 4.1 fusion.27
  915.0 3.5 fusion.13
  918.5 109.2 %all-to-all-done.4 = bf16[1,3,640,1024]{3,1,0,2:T(4,128)(2,1)} async-done(((bf16[1,3,640,1024]{3,1,0,2:T(4,128)(2,1)}), bf16[1,3,640,1024]{3,1,0,2:T(4,128)(2,1)}, u32[]{:S(2)}, u32[]{:S(2)}) %all-to-all-start.4) | async-done | bytes 3932192 | tf_op jit(solution)/shard_map/all_to_all | solution.py:107
  1027.7 4.9 all-to-all-start.3
  1032.6 7.9 fusion.16
  1040.5 4.4 copy.27
  1044.9 28.0 %all-to-all-done.3 = bf16[32,40,640]{2,1,0:T(8,128)(2,1)S(1)} async-done(((bf16[32,40,640]{2,1,0:T(8,128)(2,1)}), bf16[32,40,640]{2,1,0:T(8,128)(2,1)S(1)}, u32[]{:S(2)}, u32[]{:S(2)}) %all-to-all-start.3) | async-done | bytes 1638432 | tf_op jit(solution)/shard_map/all_to_all | solution.py:91
  1072.9 5.5 all-to-all-start.5
  1078.4 3.4 gather_fusion
  1081.8 2.1 gather.6
  1085.4 98.6 %all-to-all-done.5 = bf16[32,3,20,1024]{3,2,1,0:T(8,128)(2,1)} async-done(((bf16[32,3,20,1024]{3,2,1,0:T(8,128)(2,1)}), bf16[32,3,20,1024]{3,2,1,0:T(8,128)(2,1)}, u32[]{:S(2)}, u32[]{:S(2)}) %all-to-all-start.5) | async-done | bytes 3932192 | tf_op jit(solution)/shard_map/all_to_all | solution.py:110
  1184.0 5.2 copy.28
  1189.2 6.9 all_to_all.53
  1196.1 4.1 slice_bitcast_fusion
  (69 shorter events, 20.7 us)
Async XLA Ops:
  7.2 182.7 %copy-start = (bf16[1,640,1024]{2,1,0:T(8,128)(2,1)S(1)}, bf16[1,640,1024]{2,1,0:T(8,128)(2,1)}, u32[]{:S(2)}) copy-start(bf16[1,640,1024]{2,1,0:T(8,128)(2,1)} %param.13) | copy-start | bytes 3932164
  7.2 358.6 %all-gather.3.cloned.1.call-start = ((), (), s32[]{:S(2)}) async-start(), calls=%async_computation.6 | async-start | bytes 23592960 | tf_op jit(solution)/shard_map/all_gather | solution.py:78
  22.7 51.8 %copy-start.15 = (bf16[1,640,1024]{2,1,0:T(8,128)(2,1)S(1)}, bf16[1,640,1024]{2,1,0:T(8,128)(2,1)}, u32[]{:S(2)}) copy-start(bf16[1,640,1024]{2,1,0:T(8,128)(2,1)} %param.14) | copy-start | bytes 3932164
  73.4 1.2 copy-start.7
  78.2 0.7 copy-start.13
  78.2 14.5 %copy-start.11 = (bf16[128,640]{1,0:T(8,128)(2,1)S(1)}, bf16[128,640]{1,0:T(8,128)(2,1)}, u32[]{:S(2)}) copy-start(bf16[128,640]{1,0:T(8,128)(2,1)} %param.9) | copy-start | bytes 491524
  88.6 13.1 %all-to-all-start = ((bf16[32,1,40]{2,1,0:T(2,128)(2,1)}), bf16[32,1,40]{2,1,0:T(2,128)(2,1)S(1)}, u32[]{:S(2)}, u32[]{:S(2)}) async-start(bf16[32,1,40]{2,1,0:T(2,128)(2,1)} %all_to_all.54), calls=%async_computation | async-start | bytes 32768 | tf_op jit(solution)/shard_map/all_to_all | solution.py:61
  101.7 87.9 %all-to-all-start.1 = ((bf16[32,40,640]{2,1,0:T(8,128)(2,1)}), bf16[32,40,640]{2,1,0:T(8,128)(2,1)S(1)}, u32[]{:S(2)}, u32[]{:S(2)}) async-start(bf16[32,40,640]{2,1,0:T(8,128)(2,1)} %bitcast.90), calls=%async_computation.1 | async-start | bytes 3276800 | tf_op jit(solution)/shard_map/all_to_all | solution.py:54
  143.6 743.1 %all-reduce.3.cloned.1.call-start = ((), (), s32[]{:S(2)}) async-start(), calls=%async_computation.7 | async-start | bytes 10485760 | tf_op jit(solution)/shard_map/psum | solution.py:79
  189.5 1.6 copy-start.8
  191.1 3.7 copy-start.14
  365.8 520.9 %copy-start.10 = (bf16[1280,640]{1,0:T(8,128)(2,1)S(1)}, bf16[1280,640]{1,0:T(8,128)(2,1)}, u32[]{:S(2)}) copy-start(bf16[1280,640]{1,0:T(8,128)(2,1)} %fusion.12) | copy-start | bytes 4915204
  886.7 4.8 copy-start.1
  886.7 4.8 copy-start.2
  886.7 4.9 copy-start.3
  891.6 3.0 copy-start.9
  894.6 1.9 copy-start.4
  894.6 2.4 copy-start.6
  905.1 122.6 %all-to-all-start.4 = ((bf16[1,3,640,1024]{3,1,0,2:T(4,128)(2,1)}), bf16[1,3,640,1024]{3,1,0,2:T(4,128)(2,1)}, u32[]{:S(2)}, u32[]{:S(2)}) async-start(bf16[1,3,640,1024]{3,1,0,2:T(4,128)(2,1)} %copy.24), calls=%async_computation.4 | async-start | bytes 10485760 | tf_op jit(solution)/shard_map/all_to_all | solution.py:107
  910.9 4.2 copy-start.5
  910.9 4.2 copy-start.16
  918.5 114.1 %copy-start.12 = (s32[32]{0:T(128)S(1)}, s32[32]{0:T(128)}, u32[]{:S(2)}) copy-start(s32[32]{0:T(128)} %param.12) | copy-start | bytes 388
  1027.7 45.2 %all-to-all-start.3 = ((bf16[32,40,640]{2,1,0:T(8,128)(2,1)}), bf16[32,40,640]{2,1,0:T(8,128)(2,1)S(1)}, u32[]{:S(2)}, u32[]{:S(2)}) async-start(bf16[32,40,640]{2,1,0:T(8,128)(2,1)} %bitcast.96), calls=%async_computation.3 | async-start | bytes 3276800 | tf_op jit(solution)/shard_map/all_to_all | solution.py:91
  1072.9 111.1 %all-to-all-start.5 = ((bf16[32,3,20,1024]{3,2,1,0:T(8,128)(2,1)}), bf16[32,3,20,1024]{3,2,1,0:T(8,128)(2,1)}, u32[]{:S(2)}, u32[]{:S(2)}) async-start(bf16[32,3,20,1024]{3,2,1,0:T(8,128)(2,1)} %copy.27), calls=%async_computation.5 | async-start | bytes 9437184 | tf_op jit(solution)/shard_map/all_to_all | solution.py:110
Sparse Core Ops, SparseCore 0:
  78.4 287.3 all-gather.2
  368.5 518.1 all-reduce.2
